TPU v7x, 32 devices: a whole 2x2x4 slice. The times are simulated.
32 devices in a mesh: centre: 8 (over z, y), row: 4 (over x, core).
Axes of the slice: x: 2, y: 2, z: 4, core: 2. Of those that a mesh axis runs over, the one named last changes fastest.
Arguments:
- pool: bfloat16 [1024, 16384], P('centre', 'row')
- batch_index: int32 [1024], P('row'), may hold values from 0 to 16383, as said below
- targets: float32 [10, 1024], P(None, 'row'), may hold values from -6 to 6
- centres: bfloat16 [65536, 1024], P(('centre', 'row'))
- weights: float32 [10, 65536], P(None, ('centre', 'row')), may hold values from -0.0234375 to 0.0234375
- sample_index: int32 [512], P(('centre', 'row')), may hold values from 0 to 65535, as said below
- factor: float32 [512, 128], P(('centre', 'row')), may hold values from -0.5 to 0.5
Outputs:
- gradient: float32 [10, 1024], P(None, 'row')
- update: float32 [10, 512], P(None, ('centre', 'row'))
Inputs may be any that keep to these rules, and one draw needn't show every extreme that they name: `batch_index`: the entries at positions r * 256 to (r + 1) * 256 - 1 lie in r * 4096 to (r + 1) * 4096 - 1; repeats may occur. `sample_index`: all entries differ; the entries at positions k * 16 to (k + 1) * 16 - 1 lie in k * 2048 to (k + 1) * 2048 - 1.
All inputs are finite; a program needn't handle non-finite values.
Results may differ from a plain program's by a relative error of at most 0.0003.
Values may be sent and summed in bfloat16 or wider, within the bound.
A program may use at most 128 MiB of HBM per device.

v0:
```python
import math
import jax
import jax.numpy as jnp
from jax import lax
from jax.sharding import PartitionSpec as P

PROJ_STEPS = 2
EPS = 1e-06
HIGH = lax.Precision.HIGHEST


def row_scale(rows, axis):
    values = rows.astype(jnp.float32)
    return jnp.sqrt(jnp.mean(values * values, axis=axis) + EPS)


def tangent_kernel(inner, left_scale, right_scale, width):
    product = left_scale[:, None] * right_scale[None, :]
    cosine = jnp.clip(inner / (width * product), -1.0, 1.0)
    angle = jnp.arccos(cosine)
    first = (math.pi - angle) / math.pi
    second = (cosine * (math.pi - angle) + jnp.sqrt(1.0 - cosine * cosine)) / math.pi
    return product * (second + cosine * first)


def on_device(pool, batch_index, targets, centres, weights, sample_index, factor):
    width = float(centres.shape[1])
    labels = weights.shape[0]
    rows_dev = batch_index.shape[0]
    pool_dev = pool.shape[1]
    cent_dev = centres.shape[0]
    samp_dev = sample_index.shape[0]
    row_count = lax.axis_size("row")
    total_rows = rows_dev * row_count
    total_samp = samp_dev * row_count * lax.axis_size("centre")
    contract = (((1,), (1,)), ((), ()))
    local_batch = batch_index - lax.axis_index("row") * pool_dev
    picked = jnp.take(pool, local_batch, axis=1)
    features = lax.all_gather(picked, "centre", axis=0, tiled=True)
    all_targets = lax.all_gather(targets, "row", axis=1, tiled=True)
    centre_scale = row_scale(centres, 1)
    local_sample = sample_index - lax.axis_index(("centre", "row")) * cent_dev
    sample_rows = jnp.take(centres, local_sample, axis=0)
    sample_scale = jnp.take(centre_scale, local_sample)
    piece = lax.all_gather(features, "row", axis=1, tiled=True)
    inner = jnp.dot(centres, piece, preferred_element_type=jnp.float32)
    kernel = tangent_kernel(inner, centre_scale, row_scale(piece, 0), width)
    partial_value = jnp.dot(weights, kernel, precision=HIGH)
    tiles = jnp.concatenate([partial_value, jnp.take(kernel, local_sample, axis=0)], axis=0)
    partial_value = tiles[:labels]
    cross = tiles[labels:]
    totals = lax.psum(partial_value, ("centre", "row"))
    gradient_all = totals - all_targets
    gradient = lax.dynamic_slice_in_dim(gradient_all, lax.axis_index("row") * rows_dev, rows_dev, 1)
    push = lax.dot_general(gradient_all, cross, contract, precision=HIGH) / total_rows
    piece = lax.all_gather(sample_rows, ("centre", "row"), axis=0, tiled=True)
    inner = lax.dot_general(sample_rows, piece, contract, preferred_element_type=jnp.float32)
    block = tangent_kernel(inner, sample_scale, row_scale(piece, 1), width)
    update = jnp.zeros((labels, samp_dev), jnp.float32)
    for step in range(PROJ_STEPS):
        if step == 0:
            slope = push
        else:
            update_whole = lax.all_gather(update, ("centre", "row"), axis=1, tiled=True)
            slope = (
                lax.dot_general(update_whole, block, contract, precision=HIGH) / total_samp + push
            )
        coef = lax.psum(jnp.dot(slope, factor, precision=HIGH), ("centre", "row"))
        update = update - (slope - jnp.dot(coef, factor.T, precision=HIGH))
    return (gradient, update)


def solution(mesh):
    placed = (
        P("centre", "row"),
        P("row"),
        P(None, "row"),
        P(("centre", "row"), None),
        P(None, ("centre", "row")),
        P(("centre", "row")),
        P(("centre", "row"), None),
    )
    return jax.shard_map(
        on_device,
        mesh=mesh,
        in_specs=placed,
        out_specs=(P(None, "row"), P(None, ("centre", "row"))),
        check_vma=False,
    )
```

profile of v0, /device:TPU:10, one launch (start us, length us, event | category | flops | bytes accessed | tf_op | source)
XLA Modules:
  0.0 314.5 jit_solution(3120540883913514165)
XLA Ops:
  7.2 0.0 copy-start
  7.2 0.0 copy-start.3
  7.2 0.0 all-gather.5.cloned.1.call-start
  7.2 0.7 compare_and_fusion
  7.9 3.3 %gather_fusion.3 = bf16[16,1024]{1,0:T(8,128)(2,1)S(1)} fusion(bf16[2048,1024]{1,0:T(8,128)(2,1)} %param.10, s32[1024]{0:T(1024)S(1)} %pad_clamp_fusion), kind=kCustom, calls=%fused_computation.3 | custom fusion | bytes 65600 | tf_op jit(solution)/shard_map/jit(_take)/gather | solution.py:43
  11.3 0.7 broadcast_select_fusion
  11.9 0.0 copy-start.1
  11.9 0.0 all-gather.5.cloned.1.call-update
  12.0 0.0 all-gather.3.cloned.1.call-start
  12.0 1.6 copy.13
  13.6 0.7 compare_and_fusion.1
  14.3 0.9 gather_fusion
  15.2 0.1 select_bitcast_fusion
  15.3 28.9 %all_gather.15 = bf16[1024,256]{0,1:T(8,128)(2,1)} all-gather(bf16[128,256]{0,1:T(8,128)(2,1)S(1)} %select_bitcast_fusion), channel_id=1, replica_groups=mesh['centre'=8,'row'=4] {'centre'}, dimensions={0}, use_global_device_ids=true | all-gather | bytes 589824 | tf_op jit(solution)/shard_map/all_gather | solution.py:39
  44.2 0.0 all-gather.3.cloned.1.call-update
  44.2 3.1 multiply_reduce_fusion
  47.3 0.7 gather_fusion.2
  48.0 0.0 copy-done.3
  48.0 5.2 %all_gather.17 = f32[10,1024]{1,0:T(8,128)S(1)} all-gather(f32[10,256]{1,0:T(8,128)S(1)} %copy-done.3), channel_id=1, replica_groups=mesh['centre'=8,'row'=4] {'row'}, dimensions={1}, use_global_device_ids=true | all-gather | bytes 51200 | tf_op jit(solution)/shard_map/all_gather | solution.py:40
  53.2 13.0 %all-gather.5.cloned.1.call-done = bf16[512,1024]{1,0:T(8,128)(2,1)} async-done(((bf16[16,1024]{1,0:T(8,128)(2,1)}), bf16[512,1024]{1,0:T(8,128)(2,1)}) %all-gather.5.cloned.1.call-update) | async-done | bytes 1048592 | tf_op jit(solution)/shard_map/all_gather | solution.py:56
  66.3 1.5 multiply_reduce_fusion.2
  67.8 0.0 copy-done.1
  67.8 1.6 fusion.2
  69.4 19.9 %all-gather.3.cloned.1.call-done = bf16[1024,1024]{0,1:T(8,128)(2,1)} async-done(((bf16[1024,256]{0,1:T(8,128)(2,1)}), bf16[1024,1024]{0,1:T(8,128)(2,1)}) %all-gather.3.cloned.1.call-update) | async-done | bytes 2097168 | tf_op jit(solution)/shard_map/all_gather | solution.py:45
  89.2 2.1 multiply_reduce_fusion.1
  91.3 29.4 %multiply_multiply_fusion = f32[2048,1024]{0,1:T(8,128)} fusion(bf16[1024,1024]{0,1:T(8,128)(2,1)} %all-gather.3.cloned.1.call-done, bf16[2048,1024]{1,0:T(8,128)(2,1)} %param.10, f32[1024]{0:T(1024)S(1)} %add_sqrt_fusion.1, f32[2048]{0:T(1024)S(1)} %add_sqrt_fusion), kind=kOutput, calls=%fused_computation.4 | convolution fusion | flops 4330618880 | bytes 14692352 | tf_op jit(solution)/shard_map/dot_general | solution.py:46
  120.7 9.3 %copy.14 = f32[2048,1024]{1,0:T(8,128)} copy(f32[2048,1024]{0,1:T(8,128)} %multiply_multiply_fusion) | data formatting | bytes 16777216 | tf_op jit(solution)/shard_map/mul | solution.py:23
  129.9 0.0 copy-start.2
  129.9 4.0 %gather_fusion.1 = f32[16,1024]{1,0:T(8,128)S(1)} fusion(f32[2048,1024]{1,0:T(8,128)} %copy.14, s32[1024]{0:T(1024)S(1)} %pad_clamp_fusion), kind=kCustom, calls=%fused_computation.1 | custom fusion | bytes 131136 | tf_op jit(solution)/shard_map/jit(_take)/gather | solution.py:49
  134.0 0.0 copy-done
  134.0 9.4 %convolution_bitcast_fusion = f32[10,1024]{1,0:T(8,128)S(1)} fusion(f32[2048,1024]{0,1:T(8,128)} %multiply_multiply_fusion, f32[10,2048]{1,0:T(8,128)S(1)} %copy-done), kind=kOutput, calls=%fused_computation.11 | convolution fusion | flops 251658240 | bytes 8511488 | tf_op jit(solution)/shard_map/dot_general | solution.py:48
  143.4 41.3 %psum.21 = f32[10,1024]{1,0:T(8,128)S(1)} all-reduce(f32[10,1024]{1,0:T(8,128)S(1)} %convolution_bitcast_fusion), channel_id=1, replica_groups=mesh['centre'=8,'row'=4] {'centre','row'}, use_global_device_ids=true, to_apply=%region_2.3 | all-reduce | flops 10240 | bytes 81920 | tf_op jit(solution)/shard_map/psum | solution.py:52
  184.7 0.2 convolution_multiply_fusion.1
  185.0 0.0 copy-done.2
  185.0 0.1 fusion.33
  185.1 40.0 %psum.22 = f32[10,128]{1,0:T(8,128)S(1)} all-reduce(f32[10,128]{1,0:T(8,128)S(1)} %fusion.33), channel_id=1, replica_groups=mesh['centre'=8,'row'=4] {'centre','row'}, use_global_device_ids=true, to_apply=%region_3.4 | all-reduce | flops 1280 | bytes 10240 | tf_op jit(solution)/shard_map/psum | solution.py:68
  225.2 0.1 fusion.5
  225.3 0.1 copy.15
  225.4 31.4 %all_gather.18 = f32[10,512]{0,1:T(8,128)S(1)} all-gather(f32[10,16]{0,1:T(8,128)S(1)} %copy.15), channel_id=1, replica_groups=mesh['centre'=8,'row'=4] {'centre','row'}, dimensions={1}, use_global_device_ids=true | all-gather | bytes 21120 | tf_op jit(solution)/shard_map/all_gather | solution.py:64
  256.8 0.6 fusion.4
  257.4 0.1 fusion.34
  257.5 48.8 %psum.23 = f32[10,128]{1,0:T(8,128)S(1)} all-reduce(f32[10,128]{1,0:T(8,128)S(1)} %fusion.34), channel_id=1, replica_groups=mesh['centre'=8,'row'=4] {'centre','row'}, use_global_device_ids=true, to_apply=%region_5.6 | all-reduce | flops 1280 | bytes 10240 | tf_op jit(solution)/shard_map/psum | solution.py:68
  306.4 0.7 fusion.3
  307.1 0.6 constant_dynamic-slice_fusion
  (7 shorter events, 0.1 us)
Async XLA Ops:
  7.2 126.8 %copy-start = (f32[10,2048]{1,0:T(8,128)S(1)}, f32[10,2048]{1,0:T(8,128)}, u32[]{:S(2)}) copy-start(f32[10,2048]{1,0:T(8,128)} %param.11) | copy-start | bytes 245764
  7.2 40.8 %copy-start.3 = (f32[10,256]{1,0:T(8,128)S(1)}, f32[10,256]{1,0:T(8,128)}, u32[]{:S(2)}) copy-start(f32[10,256]{1,0:T(8,128)} %param.9) | copy-start | bytes 30724
  7.2 59.1 %all-gather.5.cloned.1.call-start = ((), (), s32[]{:S(2)}) async-start(), calls=%async_computation.1 | async-start | bytes 1081344 | tf_op jit(solution)/shard_map/all_gather | solution.py:56
  11.9 55.8 %copy-start.1 = (bf16[16,1024]{1,0:T(8,128)(2,1)S(1)}, bf16[16,1024]{1,0:T(8,128)(2,1)}, u32[]{:S(2)}) copy-start(bf16[16,1024]{1,0:T(8,128)(2,1)} %broadcast_select_fusion) | copy-start | bytes 98308
  12.0 77.3 %all-gather.3.cloned.1.call-start = ((), (), s32[]{:S(2)}) async-start(), calls=%async_computation | async-start | bytes 2621440 | tf_op jit(solution)/shard_map/all_gather | solution.py:45
  129.9 55.0 %copy-start.2 = (f32[16,128]{1,0:T(8,128)S(1)}, f32[16,128]{1,0:T(8,128)}, u32[]{:S(2)}) copy-start(f32[16,128]{1,0:T(8,128)} %param.13) | copy-start | bytes 24580
Sparse Core Ops, SparseCore 0:
  12.1 54.1 all-gather.4
  67.8 21.3 all-gather.2
where the time goes:
time: 315 us
  blocking collectives  196 us (62%)
  matrix products  42.3 us (13%)
  waiting for transfers between devices  32.9 us (10%)
  local copies, waits for them, and re-layouts  20.5 us (7%)
  between operations  14.2 us (5%)
  other arithmetic  8.84 us (3%)
    psum x2, blocking collectives, on_device(): coef = lax.psum(jnp.dot(slope, factor, precision=HIGH), ('centre', 'row'))  88.9 us
    psum x1, blocking collectives, on_device(): totals = lax.psum(partial_value, ('centre', 'row'))  41.3 us
    all_gather x1, blocking collectives, on_device(): update_whole = lax.all_gather(update, ('centre', 'row'), axis=1, tiled=True)  31.4 us
    dot_general x1, matrix products, on_device(): inner = jnp.dot(centres, piece, preferred_element_type=jnp.float32)  29.4 us
    all_gather x1, blocking collectives, on_device(): features = lax.all_gather(picked, 'centre', axis=0, tiled=True)  28.9 us
    all_gather x1, waiting for transfers between devices, on_device(): piece = lax.all_gather(features, 'row', axis=1, tiled=True)  19.9 us
    all_gather x1, waiting for transfers between devices, on_device(): piece = lax.all_gather(sample_rows, ('centre', 'row'), axis=0, tiled=True)  13 us
    dot_general x1, matrix products, on_device(): partial_value = jnp.dot(weights, kernel, precision=HIGH)  9.43 us
  transfers between devices with their start and end apart: 2, of which 2 were waited for; matrix products, arithmetic and copies ran while one was open for 3% of the time, Pallas kernels for 0%

commit v1 on v0

--- a/solution.py
+++ b/solution.py
@@ -42,7 +42,12 @@
     local_sample = sample_index - lax.axis_index(("centre", "row")) * cent_dev
     sample_rows = jnp.take(centres, local_sample, axis=0)
     sample_scale = jnp.take(centre_scale, local_sample)
-    piece = lax.all_gather(features, "row", axis=1, tiled=True)
+    ring = [features]
+    for hop in range(3):
+        ring.append(lax.ppermute(ring[-1], "row", [(dev, (dev + 1) % 4) for dev in range(4)]))
+    piece = jnp.roll(
+        jnp.concatenate(ring[::-1], axis=1), (lax.axis_index("row") + 1) * ring[0].shape[1], axis=1
+    )
     inner = jnp.dot(centres, piece, preferred_element_type=jnp.float32)
     kernel = tangent_kernel(inner, centre_scale, row_scale(piece, 0), width)
     partial_value = jnp.dot(weights, kernel, precision=HIGH)

time: 315 us -> 291 us (0.924)
  waiting for transfers between devices: 32.9 us -> 12.5 us
    all_gather x1 -> x0, waiting for transfers between devices: 19.9 us -> none  [on_device(): piece = lax.all_gather(features, 'row', axis=1, tiled=True)]
    all_gather x1, waiting for transfers between devices: 13 us -> 0.01 us  [on_device(): piece = lax.all_gather(sample_rows, ('centre', 'row'), axis=0, tiled=True)]
    ppermute x0 -> x3, waiting for transfers between devices: none -> 12.5 us  [on_device(): lax.ppermute(ring[-1], 'row', [(dev, (dev + 1) % 4) for dev in range(4)])]
  transfers between devices with their start and end apart: 2 -> 4, of which waited for: 2 -> 2; matrix products, arithmetic and copies ran while one was open for 3% -> 21% of each run, Pallas kernels for 0% -> 0%
where the time goes in v1:
time: 291 us; the launch traced here: 290 us
  blocking collectives  194 us (67%)
  matrix products  39.8 us (14%)
  local copies, waits for them, and re-layouts  22.2 us (8%)
  between operations  14.3 us (5%)
  waiting for transfers between devices  12.5 us (4%)
  other arithmetic  7.25 us (2%)
    psum x2, blocking collectives, on_device(): coef = lax.psum(jnp.dot(slope, factor, precision=HIGH), ('centre', 'row'))  88.5 us
    psum x1, blocking collectives, on_device(): totals = lax.psum(partial_value, ('centre', 'row'))  41.1 us
    all_gather x1, blocking collectives, on_device(): update_whole = lax.all_gather(update, ('centre', 'row'), axis=1, tiled=True)  31.3 us
    all_gather x1, blocking collectives, on_device(): features = lax.all_gather(picked, 'centre', axis=0, tiled=True)  26.9 us
    dot_general x1, matrix products, on_device(): inner = jnp.dot(centres, piece, preferred_element_type=jnp.float32)  26.9 us
    ppermute x3, waiting for transfers between devices, on_device(): lax.ppermute(ring[-1], 'row', [(dev, (dev + 1) % 4) for dev in range(4)])  12.5 us
    dot_general x1, matrix products, on_device(): partial_value = jnp.dot(weights, kernel, precision=HIGH)  9.43 us
    mul x1, local copies, waits for them, and re-layouts, tangent_kernel(): return product * (second + cosine * first)  9.27 us
  transfers between devices with their start and end apart: 4, of which 2 were waited for; matrix products, arithmetic and copies ran while one was open for 21% of the time, Pallas kernels for 0%

profile of v1, /device:TPU:10, one launch (start us, length us, event | category | flops | bytes accessed | tf_op | source)
XLA Modules:
  0.0 290.2 jit_solution(17802373818850747467)
XLA Ops:
  7.2 0.0 copy-start
  7.2 0.0 all-gather.2.cloned.1.call-start
  7.2 0.7 compare_and_fusion.1
  7.9 0.0 copy-start.4
  7.9 1.6 copy.13
  9.6 0.9 gather_fusion
  10.4 0.1 select_bitcast_fusion
  10.5 26.9 %all_gather.12 = bf16[1024,256]{0,1:T(8,128)(2,1)S(1)} all-gather(bf16[128,256]{0,1:T(8,128)(2,1)S(1)} %select_bitcast_fusion), channel_id=1, replica_groups=mesh['centre'=8,'row'=4] {'centre'}, dimensions={0}, use_global_device_ids=true | all-gather | bytes 589824 | tf_op jit(solution)/shard_map/all_gather | solution.py:39
  37.5 0.0 collective-permute-start
  37.5 8.6 %collective-permute-done = bf16[1024,256]{0,1:T(8,128)(2,1)S(1)} collective-permute-done((bf16[1024,256]{0,1:T(8,128)(2,1)S(1)}, bf16[1024,256]{0,1:T(8,128)(2,1)S(1)}, u32[]{:S(2)}, u32[]{:S(2)}) %collective-permute-start) | collective-permute-done | bytes 524320 | tf_op jit(solution)/shard_map/ppermute | solution.py:47
  46.1 0.0 collective-permute-start.1
  46.1 0.7 compare_and_fusion
  46.8 3.3 %gather_fusion.3 = bf16[16,1024]{1,0:T(8,128)(2,1)S(1)} fusion(bf16[2048,1024]{1,0:T(8,128)(2,1)} %param.10, s32[1024]{0:T(1024)S(1)} %pad_clamp_fusion), kind=kCustom, calls=%fused_computation.3 | custom fusion | bytes 65600 | tf_op jit(solution)/shard_map/jit(_take)/gather | solution.py:43
  50.1 0.7 broadcast_select_fusion
  50.8 0.0 all-gather.2.cloned.1.call-update
  50.8 3.9 %collective-permute-done.1 = bf16[1024,256]{0,1:T(8,128)(2,1)S(1)} collective-permute-done((bf16[1024,256]{0,1:T(8,128)(2,1)S(1)}, bf16[1024,256]{0,1:T(8,128)(2,1)S(1)}, u32[]{:S(2)}, u32[]{:S(2)}) %collective-permute-start.1) | collective-permute-done | bytes 524320 | tf_op jit(solution)/shard_map/ppermute | solution.py:47
  54.7 0.0 collective-permute-start.2
  54.7 3.1 %multiply_reduce_fusion = f32[2048]{0:T(1024)S(1)} fusion(bf16[2048,1024]{1,0:T(8,128)(2,1)} %param.10), kind=kLoop, calls=%fused_computation.8 | loop fusion | flops 6289408 | bytes 4202496 | tf_op jit(solution)/shard_map/reduce_sum | solution.py:14
  57.8 0.7 gather_fusion.2
  58.5 0.0 copy-done.4
  58.5 6.3 %all_gather.13 = f32[10,1024]{1,0:T(8,128)S(1)} all-gather(f32[10,256]{1,0:T(8,128)S(1)} %copy-done.4), channel_id=1, replica_groups=mesh['centre'=8,'row'=4] {'row'}, dimensions={1}, use_global_device_ids=true | all-gather | bytes 51200 | tf_op jit(solution)/shard_map/all_gather | solution.py:40
  64.8 0.0 collective-permute-done.2
  64.9 0.0 copy-start.1
  65.1 0.5 multiply_reduce_fusion.1
  65.6 1.4 copy-done.1
  67.1 26.9 %multiply_multiply_fusion = f32[2048,1024]{0,1:T(8,128)} fusion(bf16[2048,1024]{1,0:T(8,128)(2,1)S(1)} %copy-done.1, f32[1024]{0:T(1024)S(1)} %add_sqrt_fusion.1, f32[2048]{0:T(1024)S(1)} %add_sqrt_fusion, bf16[1024,2048]{0,1:T(8,128)(2,1)S(1)} %constant_dynamic-update-slice_fusion, s32[]{:T(128)S(6)} %select_n.51), kind=kOutput, calls=%fused_computation.4 | convolution fusion | flops 4330618880 | bytes 14692356 | tf_op jit(solution)/shard_map/dot_general | solution.py:51
  93.9 9.3 %copy.14 = f32[2048,1024]{1,0:T(8,128)} copy(f32[2048,1024]{0,1:T(8,128)} %multiply_multiply_fusion) | data formatting | bytes 16777216 | tf_op jit(solution)/shard_map/mul | solution.py:23
  103.2 4.0 %gather_fusion.1 = f32[16,1024]{1,0:T(8,128)S(1)} fusion(f32[2048,1024]{1,0:T(8,128)} %copy.14, s32[1024]{0:T(1024)S(1)} %pad_clamp_fusion), kind=kCustom, calls=%fused_computation.1 | custom fusion | bytes 131136 | tf_op jit(solution)/shard_map/jit(_take)/gather | solution.py:54
  107.2 0.0 copy-done
  107.2 0.0 copy-start.3
  107.2 0.0 copy-start.2
  107.2 9.4 %convolution_bitcast_fusion = f32[10,1024]{1,0:T(8,128)S(1)} fusion(f32[2048,1024]{0,1:T(8,128)} %multiply_multiply_fusion, f32[10,2048]{1,0:T(8,128)S(1)} %copy-done), kind=kOutput, calls=%fused_computation.12 | convolution fusion | flops 251658240 | bytes 8511488 | tf_op jit(solution)/shard_map/dot_general | solution.py:53
  116.7 41.1 %psum.21 = f32[10,1024]{1,0:T(8,128)S(1)} all-reduce(f32[10,1024]{1,0:T(8,128)S(1)} %convolution_bitcast_fusion), channel_id=1, replica_groups=mesh['centre'=8,'row'=4] {'centre','row'}, use_global_device_ids=true, to_apply=%region_2.3 | all-reduce | flops 10240 | bytes 81920 | tf_op jit(solution)/shard_map/psum | solution.py:57
  157.8 0.2 convolution_multiply_fusion.1
  158.0 0.0 copy-done.3
  158.0 0.1 fusion.35
  158.2 39.4 %psum.22 = f32[10,128]{1,0:T(8,128)S(1)} all-reduce(f32[10,128]{1,0:T(8,128)S(1)} %fusion.35), channel_id=1, replica_groups=mesh['centre'=8,'row'=4] {'centre','row'}, use_global_device_ids=true, to_apply=%region_3.4 | all-reduce | flops 1280 | bytes 10240 | tf_op jit(solution)/shard_map/psum | solution.py:73
  197.6 0.1 fusion.6
  197.7 0.1 copy.15
  197.8 31.3 %all_gather.14 = f32[10,512]{0,1:T(8,128)S(1)} all-gather(f32[10,16]{0,1:T(8,128)S(1)} %copy.15), channel_id=1, replica_groups=mesh['centre'=8,'row'=4] {'centre','row'}, dimensions={1}, use_global_device_ids=true | all-gather | bytes 21120 | tf_op jit(solution)/shard_map/all_gather | solution.py:69
  229.1 0.6 constant_dynamic-slice_fusion
  229.7 0.0 all-gather.2.cloned.1.call-done
  229.7 1.5 multiply_reduce_fusion.2
  231.2 0.0 copy-done.2
  231.2 1.6 fusion.3
  232.8 0.6 fusion.5
  233.4 0.1 fusion.36
  233.5 49.1 %psum.23 = f32[10,128]{1,0:T(8,128)S(1)} all-reduce(f32[10,128]{1,0:T(8,128)S(1)} %fusion.36), channel_id=1, replica_groups=mesh['centre'=8,'row'=4] {'centre','row'}, use_global_device_ids=true, to_apply=%region_5.6 | all-reduce | flops 1280 | bytes 10240 | tf_op jit(solution)/shard_map/psum | solution.py:73
  282.6 0.7 fusion.4
  (15 shorter events, 0.3 us)
Async XLA Ops:
  7.2 100.0 %copy-start = (f32[10,2048]{1,0:T(8,128)S(1)}, f32[10,2048]{1,0:T(8,128)}, u32[]{:S(2)}) copy-start(f32[10,2048]{1,0:T(8,128)} %param.11) | copy-start | bytes 245764
  7.2 222.5 %all-gather.2.cloned.1.call-start = ((), (), s32[]{:S(2)}) async-start(), calls=%async_computation | async-start | bytes 1081344 | tf_op jit(solution)/shard_map/all_gather | solution.py:61
  7.9 50.5 %copy-start.4 = (f32[10,256]{1,0:T(8,128)S(1)}, f32[10,256]{1,0:T(8,128)}, u32[]{:S(2)}) copy-start(f32[10,256]{1,0:T(8,128)} %param.9) | copy-start | bytes 30724
  37.5 8.6 %collective-permute-start = (bf16[1024,256]{0,1:T(8,128)(2,1)S(1)}, bf16[1024,256]{0,1:T(8,128)(2,1)S(1)}, u32[]{:S(2)}, u32[]{:S(2)}) collective-permute-start(bf16[1024,256]{0,1:T(8,128)(2,1)S(1)} %all_gather.12), channel_id=1, source_target_pairs={{0,1},{1,2},{2,3},{3,0},{4,5},{5,6},{6,7},{7,4},{8,9},{9,10},{10,1... | collective-permute-start | bytes 1572872 | tf_op jit(solution)/shard_map/ppermute | solution.py:47
  46.1 8.6 %collective-permute-start.1 = (bf16[1024,256]{0,1:T(8,128)(2,1)S(1)}, bf16[1024,256]{0,1:T(8,128)(2,1)S(1)}, u32[]{:S(2)}, u32[]{:S(2)}) collective-permute-start(bf16[1024,256]{0,1:T(8,128)(2,1)S(1)} %collective-permute-done), channel_id=1, source_target_pairs={{0,1},{1,2},{2,3},{3,0},{4,5},{5,6},{6,7},{7,4},{8,9},{9,10},{10,1... | collective-permute-start | bytes 1572872 | tf_op jit(solution)/shard_map/ppermute | solution.py:47
  54.7 10.1 %collective-permute-start.2 = (bf16[1024,256]{0,1:T(8,128)(2,1)S(1)}, bf16[1024,256]{0,1:T(8,128)(2,1)S(1)}, u32[]{:S(2)}, u32[]{:S(2)}) collective-permute-start(bf16[1024,256]{0,1:T(8,128)(2,1)S(1)} %collective-permute-done.1), channel_id=1, source_target_pairs={{0,1},{1,2},{2,3},{3,0},{4,5},{5,6},{6,7},{7,4},{8,9},{9,10},{10,1... | collective-permute-start | bytes 1572872 | tf_op jit(solution)/shard_map/ppermute | solution.py:47
  64.9 2.2 copy-start.1
  107.2 50.8 %copy-start.3 = (f32[16,128]{1,0:T(8,128)S(1)}, f32[16,128]{1,0:T(8,128)}, u32[]{:S(2)}) copy-start(f32[16,128]{1,0:T(8,128)} %param.13) | copy-start | bytes 24580
  107.2 124.0 %copy-start.2 = (bf16[16,1024]{1,0:T(8,128)(2,1)S(1)}, bf16[16,1024]{1,0:T(8,128)(2,1)}, u32[]{:S(2)}) copy-start(bf16[16,1024]{1,0:T(8,128)(2,1)} %broadcast_select_fusion) | copy-start | bytes 98308
Sparse Core Ops, SparseCore 0:
  50.9 53.4 all-gather.1
